TPU v7x, 256 devices: a whole 4x4x8 slice. The times are simulated.
256 devices in a mesh: wide: 32 (over x, z_lo, y), narrow: 8 (over z_hi, core).
Axes of the slice: x: 4, y: 4, z: 8 (z_hi: 4, z_lo: 2; z = z_hi * 2 + z_lo), core: 2. Of those that a mesh axis runs over, the one named last changes fastest.
Arguments:
- volume: bfloat16 [1, 8, 128, 1024], P(None, None, 'wide', 'narrow'), may hold values from -6 to 6
- w_enter: bfloat16 [27, 32, 1], replicated, may hold values from -1.25 to 1.25
- gain_enter: float32 [32], replicated, may hold values from 0.25 to 1.75
- shift_enter: float32 [32], replicated, may hold values from -2.5 to 2.5
- w_encode: bfloat16 [27, 32, 32], replicated, may hold values from -0.21875 to 0.21875
- gain_encode: float32 [32], replicated, may hold values from 0.25 to 1.75
- shift_encode: float32 [32], replicated, may hold values from -2.5 to 2.5
- w_widen: bfloat16 [27, 64, 32], replicated, may hold values from -0.21875 to 0.21875
- gain_widen: float32 [64], replicated, may hold values from 0.25 to 1.75
- shift_widen: float32 [64], replicated, may hold values from -2.5 to 2.5
- w_deep: bfloat16 [27, 64, 64], replicated, may hold values from -0.15625 to 0.15625
- gain_deep: float32 [64], replicated, may hold values from 0.25 to 1.75
- shift_deep: float32 [64], replicated, may hold values from -2.5 to 2.5
- w_upward: bfloat16 [8, 32, 64], replicated, may hold values from -0.75 to 0.75
- w_decode: bfloat16 [27, 32, 64], replicated, may hold values from -0.15625 to 0.15625
- gain_decode: float32 [32], replicated, may hold values from 0.25 to 1.75
- shift_decode: float32 [32], replicated, may hold values from -2.5 to 2.5
- w_classes: bfloat16 [2, 32], replicated, may hold values from -1 to 1
- bias_classes: float32 [2], replicated, may hold values from -2.5 to 2.5
Outputs:
- logits: float32 [2, 8, 128, 1024], P(None, None, 'wide', 'narrow')
All inputs are finite; a program needn't handle non-finite values.
Results may differ from a plain program's by a relative error of at most 0.0054.
Values may be sent and summed in bfloat16 or wider, within the bound.
A program may use at most 64 MiB of HBM per device.

v0:
```python
import functools

import jax
import jax.numpy as jnp
from jax import lax
from jax.experimental import pallas as pl
from jax.experimental.pallas import tpu as pltpu
from jax.sharding import PartitionSpec as P

F32 = jnp.float32
BF16 = jnp.bfloat16
MESH = pl.DeviceIdType.MESH

DEPTH = 8
ROWS = 4
COLS = 128
HALF = 64
XC = 80
OFFSETS = [
    (dy, dx) for dy in (-2, 2, -1, 1, 0) for dx in (-1, 1, 0) if (dy, dx) != (0, 0)
]
POOL_PLANE = (0, 2, 1, 3)


def iota(shape, dim):
    return lax.broadcasted_iota(jnp.int32, shape, dim)


def dot(a, b):
    return jnp.dot(a, b, preferred_element_type=F32)


def dot_nt(a, b):
    return lax.dot_general(a, b, (((1,), (1,)), ((), ())), preferred_element_type=F32)


def eye(n):
    return (iota((n, n), 0) == iota((n, n), 1)).astype(BF16)


def repeat_matrix(n, total, dtype):
    return (iota((n, total), 0) == lax.rem(iota((n, total), 1), n)).astype(dtype)


def band(lane, width, tile, plane, taps):
    group = lane // width
    first = plane - tile * (128 // width)
    out = jnp.zeros(taps[0].shape, F32)
    for dz in range(3):
        place = first + 1 - dz
        if 0 <= place < 128 // width:
            out = jnp.where(group == place, taps[dz], out)
    return out


def kernel(
    n_wide,
    n_narrow,
    volume,
    w_enter,
    w_encode,
    w_widen,
    w_deep,
    w_upward,
    w_decode,
    w_classes,
    gain_enter,
    shift_enter,
    gain_encode,
    shift_encode,
    gain_widen,
    shift_widen,
    gain_deep,
    shift_deep,
    gain_decode,
    shift_decode,
    bias,
    out,
    v_volume,
    v_enter,
    v_encode,
    v_widen,
    v_deep,
    v_upward,
    v_decode,
    v_classes,
    v_gain_enter,
    v_shift_enter,
    v_gain_encode,
    v_shift_encode,
    v_gain_widen,
    v_shift_widen,
    v_gain_deep,
    v_shift_deep,
    v_gain_decode,
    v_shift_decode,
    s_bias,
    plane_rows,
    own,
    halo,
    m_enter,
    m_encode,
    m_widen,
    m_deep,
    m_upward,
    m_decode,
    first,
    skip,
    pooled,
    widened,
    lifted,
    decoded,
    load_sem,
    send_sem,
    recv_sem,
):
    w = lax.axis_index("wide")
    n = lax.axis_index("narrow")

    def partner(offset):
        return (
            lax.rem(w + offset[0] + n_wide, n_wide),
            lax.rem(n + offset[1] + n_narrow, n_narrow),
        )

    barrier = pltpu.get_barrier_semaphore()
    for offset in OFFSETS:
        pl.semaphore_signal(barrier, inc=1, device_id=partner(offset), device_id_type=MESH)

    sources = (
        volume, w_enter, w_encode, w_widen, w_deep, w_upward, w_decode, w_classes,
        gain_enter, shift_enter, gain_encode, shift_encode, gain_widen, shift_widen,
        gain_deep, shift_deep, gain_decode, shift_decode, bias,
    )
    targets = (
        v_volume, v_enter, v_encode, v_widen, v_deep, v_upward, v_decode, v_classes,
        v_gain_enter, v_shift_enter, v_gain_encode, v_shift_encode, v_gain_widen, v_shift_widen,
        v_gain_deep, v_shift_deep, v_gain_decode, v_shift_decode, s_bias,
    )
    loads = [
        pltpu.make_async_copy(source, target, load_sem.at[k])
        for k, (source, target) in enumerate(zip(sources, targets))
    ]
    for load in loads:
        load.start()

    loads[0].wait()
    for z in range(DEPTH):
        plane_rows[ROWS * z : ROWS * (z + 1), :] = v_volume[z].astype(F32)
    by_row = jnp.concatenate(
        [plane_rows[pl.ds(y, DEPTH, stride=ROWS), :] for y in range(ROWS)], axis=0
    )
    by_row = pltpu.roll(by_row, HALF, 1).astype(BF16)
    own[...] = by_row
    halo[1, 64:96, :] = by_row

    pl.semaphore_wait(barrier, len(OFFSETS))
    sends = []
    for k, offset in enumerate(OFFSETS):
        send = pltpu.make_async_remote_copy(
            src_ref=own,
            dst_ref=halo.at[1 - offset[1], pl.ds(32 * (2 - offset[0]), 32)],
            send_sem=send_sem.at[k],
            recv_sem=recv_sem.at[k],
            device_id=partner(offset),
            device_id_type=MESH,
        )
        send.start()
        sends.append(send)

    for load in loads[1:]:
        load.wait()

    def rows_of(refs):
        return jnp.concatenate([ref[...].reshape(1, ref.shape[0]) for ref in refs], axis=0)

    fine = jnp.dot(
        rows_of((v_gain_enter, v_shift_enter, v_gain_encode, v_shift_encode, v_gain_decode, v_shift_decode)),
        repeat_matrix(32, 256, F32),
        preferred_element_type=F32,
        precision=lax.Precision.HIGHEST,
    )
    coarse = jnp.dot(
        rows_of((v_gain_widen, v_shift_widen, v_gain_deep, v_shift_deep)),
        repeat_matrix(64, 256, F32),
        preferred_element_type=F32,
        precision=lax.Precision.HIGHEST,
    )

    taps = dot(v_enter[...], repeat_matrix(32, 256, BF16))
    offset_of = iota((DEPTH, 256), 0) - iota((DEPTH, 256), 1) // 32 + 1
    zero = jnp.zeros((DEPTH, 256), F32)
    blocks = {}
    for dx in range(3):
        for dy in range(3):
            block = zero
            for dz in range(3):
                row = 9 * dz + 3 * dy + dx
                block = jnp.where(
                    offset_of == dz, jnp.broadcast_to(taps[row : row + 1], (DEPTH, 256)), block
                )
            blocks[dx, dy] = block
    for yo in range(6):
        for px in range(2):
            pieces = [
                blocks.get((s - px, yin - yo), zero) for s in range(4) for yin in range(8)
            ]
            m_enter[yo, px] = jnp.concatenate(pieces, axis=0).astype(BF16)

    eye32 = eye(32)
    eye64 = eye(64)
    lane32 = iota((32, 128), 1)
    lane64 = iota((64, 128), 1)

    def build_fine(tap, carry):
        rows = [v_encode[9 * dz + tap] for dz in range(3) for _ in range(4)]
        turned = dot_nt(eye32, jnp.concatenate(rows, axis=0))
        parts = [turned[:, 128 * dz : 128 * (dz + 1)] for dz in range(3)]
        for z in range(DEPTH):
            for tile in range(2):
                m_encode[tap, 32 * z : 32 * (z + 1), 128 * tile : 128 * (tile + 1)] = band(
                    lane32, 32, tile, z, parts
                ).astype(BF16)
        rows = [v_decode[9 * dz + tap] for dz in range(3) for _ in range(4)]
        turned = dot_nt(eye64, jnp.concatenate(rows, axis=0))
        for source in range(2):
            parts = [
                turned[32 * source : 32 * (source + 1), 128 * dz : 128 * (dz + 1)]
                for dz in range(3)
            ]
            for z in range(DEPTH):
                for tile in range(2):
                    m_decode[
                        tap, source, 32 * z : 32 * (z + 1), 128 * tile : 128 * (tile + 1)
                    ] = band(lane32, 32, tile, z, parts).astype(BF16)
        return carry

    lax.fori_loop(0, 9, build_fine, 0)

    repeat64 = repeat_matrix(64, 128, BF16)

    def build_coarse(tap, carry):
        rows = [v_widen[9 * dz + tap] for dz in range(3)]
        turned = dot(jnp.concatenate(rows, axis=0), repeat64)
        parts = [turned[32 * dz : 32 * (dz + 1)] for dz in range(3)]
        for group in range(4):
            for tile in range(2):
                m_widen[tap, 32 * group : 32 * (group + 1), 128 * tile : 128 * (tile + 1)] = band(
                    lane32, 64, tile, POOL_PLANE[group], parts
                ).astype(BF16)
        rows = [v_deep[9 * dz + tap] for dz in range(3) for _ in range(2)]
        turned = dot_nt(eye64, jnp.concatenate(rows, axis=0))
        parts = [turned[:, 128 * dz : 128 * (dz + 1)] for dz in range(3)]
        for z in range(4):
            for tile in range(2):
                m_deep[tap, 64 * z : 64 * (z + 1), 128 * tile : 128 * (tile + 1)] = band(
                    lane64, 64, tile, z, parts
                ).astype(BF16)
        return carry

    lax.fori_loop(0, 9, build_coarse, 0)

    def build_upward(tap, carry):
        rows = [v_upward[4 * a + tap] for _ in range(2) for a in range(2)]
        turned = dot_nt(eye64, jnp.concatenate(rows, axis=0))
        for z in range(4):
            for tile in range(2):
                m_upward[tap, 64 * z : 64 * (z + 1), 128 * tile : 128 * (tile + 1)] = jnp.where(
                    lane64 // 64 == z - 2 * tile, turned, 0.0
                ).astype(BF16)
        return carry

    lax.fori_loop(0, 4, build_upward, 0)

    classes = dot(v_classes[...], repeat_matrix(32, 256, BF16))
    at_row = iota((64, 256), 0)
    at_lane = iota((64, 256), 1)
    per_class = jnp.where(
        at_row < 32,
        jnp.broadcast_to(classes[0:1], (64, 256)),
        jnp.broadcast_to(classes[1:2], (64, 256)),
    )
    per_plane = jnp.where(lax.rem(at_row, 32) // 4 == at_lane // 32, per_class, 0.0)
    m_classes = jnp.concatenate(
        [jnp.where(lax.rem(at_row, 4) == y, per_plane, 0.0) for y in range(ROWS)], axis=1
    ).astype(BF16)

    def inside(at, count):
        return jnp.logical_and(at >= 0, at < count).astype(F32)

    left = inside(n - 1, n_narrow)
    right = inside(n + 1, n_narrow)

    def relu_inside(acc, gain, shift, keep):
        gain = gain * keep
        shift = shift * keep
        return jnp.concatenate(
            [
                jnp.maximum(acc[0:64] * gain + shift, 0.0),
                jnp.maximum(acc[64:72] * (gain * right) + shift * right, 0.0),
                jnp.maximum(acc[72:80] * (gain * left) + shift * left, 0.0),
            ],
            axis=0,
        )

    def put_columns(ref, row, parity, value):
        ref[1 + parity, row] = value.astype(BF16)
        if parity == 0:
            ref[3, row] = pltpu.roll(value, XC - 1, 0).astype(BF16)
        else:
            ref[0, row] = pltpu.roll(value, 1, 0).astype(BF16)

    for send in sends:
        send.wait()

    lane = iota((32, 128), 1)
    wide_rows = []
    for block in range(5):
        keep = inside(w + block - 2, n_wide)
        rows = pl.ds(32 * block, 32)
        middle = halo[1, rows, :].astype(F32) * keep
        before = halo[0, rows, :].astype(F32) * (keep * left)
        after = halo[2, rows, :].astype(F32) * (keep * right)
        wide_rows.append(
            jnp.concatenate(
                [jnp.where(lane < HALF, before, middle), jnp.where(lane < HALF, middle, after)],
                axis=1,
            )
        )
    wide_rows = jnp.concatenate(wide_rows, axis=0)
    shifted = [
        (wide_rows if s == 1 else pltpu.roll(wide_rows, (1 - s) % 256, 1)).astype(BF16)
        for s in range(4)
    ]
    at = iota((XC, 256), 0)
    pick = (
        iota((XC, 256), 1) == 2 * jnp.where(at < 72, at, at - XC) + HALF
    ).astype(BF16)
    columns = jnp.concatenate(
        [
            dot_nt(
                pick, jnp.concatenate([piece[48 * g : 48 * g + 64] for piece in shifted], axis=0)
            ).astype(BF16)
            for g in range(3)
        ],
        axis=0,
    )

    for yo in range(6):
        for px in range(2):
            acc = dot(columns, m_enter[yo, px])
            for g in range(3):
                row = 6 * g + yo
                keep = inside(w * ROWS - 7 + row, n_wide * ROWS)
                put_columns(
                    first, row, px,
                    relu_inside(acc[XC * g : XC * (g + 1)], fine[0:1], fine[1:2], keep),
                )

    matrix = m_encode[...].reshape(9 * 256, 256)
    parity_acc = []
    for px in range(2):
        pieces = [
            first[px + dx, dy : dy + 16].reshape(16 * XC, 256)
            for dy in range(3)
            for dx in range(3)
        ]
        parity_acc.append(dot(jnp.concatenate(pieces, axis=1), matrix))
    pool_lane = lax.rem(iota((XC, 128), 1), 64) < 32
    for k in range(8):
        keep = inside(w * 2 - 3 + k, n_wide * 2)
        best = None
        for y in range(2):
            row = 2 * k + y
            for px in range(2):
                value = relu_inside(
                    parity_acc[px][XC * row : XC * (row + 1)], fine[2:3], fine[3:4], keep
                )
                if 5 <= row <= 10:
                    put_columns(skip, row - 5, px, value)
                best = value if best is None else jnp.maximum(best, value)
        low = best[:, 0:128]
        high = best[:, 128:256]
        low = jnp.maximum(low, pltpu.roll(low, 96, 1))
        high = jnp.maximum(high, pltpu.roll(high, 96, 1))
        best = jnp.where(pool_lane, low, pltpu.roll(high, 32, 1))
        pooled[0, k] = pltpu.roll(best, 1, 0).astype(BF16)
        pooled[1, k] = best.astype(BF16)
        pooled[2, k] = pltpu.roll(best, XC - 1, 0).astype(BF16)

    pieces = [
        pooled[dx, dy : dy + 6].reshape(6 * XC, 128) for dy in range(3) for dx in range(3)
    ]
    acc = dot(jnp.concatenate(pieces, axis=1), m_widen[...].reshape(9 * 128, 256))
    for k in range(6):
        keep = inside(w * 2 - 2 + k, n_wide * 2)
        value = relu_inside(acc[XC * k : XC * (k + 1)], coarse[0:1], coarse[1:2], keep)
        widened[0, k] = pltpu.roll(value, 1, 0).astype(BF16)
        widened[1, k] = value.astype(BF16)
        widened[2, k] = pltpu.roll(value, XC - 1, 0).astype(BF16)

    pieces = [
        widened[dx, dy : dy + 4].reshape(4 * XC, 256) for dy in range(3) for dx in range(3)
    ]
    acc = dot(jnp.concatenate(pieces, axis=1), m_deep[...].reshape(9 * 256, 256))
    deepest = jnp.concatenate(
        [
            relu_inside(
                acc[XC * k : XC * (k + 1)],
                coarse[2:3],
                coarse[3:4],
                inside(w * 2 - 1 + k, n_wide * 2),
            )
            for k in range(4)
        ],
        axis=0,
    ).astype(BF16)

    for b in range(2):
        source = deepest[XC * (1 - b) : XC * (4 - b)]
        for e in range(2):
            acc = dot(source, m_upward[2 * b + e])
            for k in range(3):
                put_columns(lifted, 2 * k + 1 - b, e, acc[XC * k : XC * (k + 1)])

    parities = []
    for px in range(2):
        pieces = [
            ref[px + dx, dy : dy + ROWS, 0:HALF].reshape(ROWS * HALF, 256)
            for dy in range(3)
            for dx in range(3)
            for ref in (skip, lifted)
        ]
        parities.append(jnp.concatenate(pieces, axis=1))
    acc = dot(jnp.concatenate(parities, axis=0), m_decode[...].reshape(18 * 256, 256))
    value = jnp.maximum(acc * fine[4:5] + fine[5:6], 0.0)
    for px in range(2):
        for y in range(ROWS):
            start = (px * ROWS + y) * HALF
            for tile in range(2):
                decoded[tile, pl.ds(y * COLS + px, HALF, stride=2), :] = value[
                    start : start + HALF, 128 * tile : 128 * (tile + 1)
                ]

    features = jnp.concatenate(
        [
            decoded[tile, y * COLS : (y + 1) * COLS, :].astype(BF16)
            for y in range(ROWS)
            for tile in range(2)
        ],
        axis=1,
    )
    logits = dot_nt(m_classes, features)
    out[...] = logits + jnp.where(iota((64, 128), 0) < 32, s_bias[0], s_bias[1])


def per_device(
    n_wide,
    n_narrow,
    volume,
    w_enter,
    gain_enter,
    shift_enter,
    w_encode,
    gain_encode,
    shift_encode,
    w_widen,
    gain_widen,
    shift_widen,
    w_deep,
    gain_deep,
    shift_deep,
    w_upward,
    w_decode,
    gain_decode,
    shift_decode,
    w_classes,
    bias_classes,
):
    operands = (
        volume.reshape(DEPTH, ROWS, COLS),
        w_enter.reshape(27, 32),
        w_encode,
        jnp.transpose(w_widen, (0, 2, 1)),
        w_deep,
        w_upward,
        w_decode,
        w_classes,
        gain_enter,
        shift_enter,
        gain_encode,
        shift_encode,
        gain_widen,
        shift_widen,
        gain_deep,
        shift_deep,
        gain_decode,
        shift_decode,
        bias_classes,
    )
    copies = [pltpu.VMEM(x.shape, x.dtype) for x in operands[:-1]]
    copies.append(pltpu.SMEM((2,), F32))
    logits = pl.pallas_call(
        functools.partial(kernel, n_wide, n_narrow),
        out_shape=jax.ShapeDtypeStruct((64, COLS), F32),
        in_specs=[pl.BlockSpec(memory_space=pltpu.HBM)] * len(operands),
        out_specs=pl.BlockSpec(memory_space=pltpu.VMEM),
        scratch_shapes=copies
        + [
            pltpu.VMEM((32, COLS), F32),
            pltpu.VMEM((32, COLS), BF16),
            pltpu.VMEM((3, 160, COLS), BF16),
            pltpu.VMEM((6, 2, 256, 256), BF16),
            pltpu.VMEM((9, 256, 256), BF16),
            pltpu.VMEM((9, 128, 256), BF16),
            pltpu.VMEM((9, 256, 256), BF16),
            pltpu.VMEM((4, 256, 256), BF16),
            pltpu.VMEM((9, 2, 256, 256), BF16),
            pltpu.VMEM((4, 18, XC, 256), BF16),
            pltpu.VMEM((4, 6, XC, 256), BF16),
            pltpu.VMEM((3, 8, XC, 128), BF16),
            pltpu.VMEM((3, 6, XC, 256), BF16),
            pltpu.VMEM((4, 6, XC, 256), BF16),
            pltpu.VMEM((2, ROWS * COLS, 128), F32),
            pltpu.SemaphoreType.DMA((len(operands),)),
            pltpu.SemaphoreType.DMA((len(OFFSETS),)),
            pltpu.SemaphoreType.DMA((len(OFFSETS),)),
        ],
        compiler_params=pltpu.CompilerParams(
            collective_id=0, has_side_effects=True, vmem_limit_bytes=52 * 1024 * 1024
        ),
        name="unet",
    )(*[pltpu.with_memory_space_constraint(x, pltpu.HBM) for x in operands])
    return logits.reshape(2, DEPTH, ROWS, COLS)


def solution(mesh):
    in_specs = (P(None, None, "wide", "narrow"),) + (P(),) * 18
    return jax.shard_map(
        functools.partial(per_device, mesh.shape["wide"], mesh.shape["narrow"]),
        mesh=mesh,
        in_specs=in_specs,
        out_specs=P(None, None, "wide", "narrow"),
        check_vma=False,
    )
```

profile of v0, /device:TPU:1, one launch (start us, length us, event | category | flops | bytes accessed | tf_op | source)
XLA Modules:
  0.0 26.1 jit_solution(17158422534314297856)
XLA Ops:
  0.0 25.5 %unet.1 = f32[64,128]{1,0:T(8,128)S(1)} custom-call(bf16[8,4,128]{2,1,0:T(4,128)(2,1)} %bitcast.6, bf16[27,32]{1,0:T(8,128)(2,1)} %bitcast.7, bf16[27,32,32]{2,1,0:T(8,128)(2,1)} %w_encode.1, bf16[27,32,64]{2,1,0:T(8,128)(2,1)} %bitcast.5, bf16[27,64,64]{2,1,0:T(8,128)(2,1)} %w_deep.1, bf16[8,32,64]{2,1,0:T(8,128)(2,1)} %w_upward.1, ...), custom_call_target="tpu_custom_call" | custom-call | tf_op jit(solution)/shard_map/unet/pallas_call | solution.py:503
  25.5 0.6 %copy.21 = f32[2,8,4,128]{3,2,1,0:T(4,128)} copy(f32[2,8,4,128]{3,2,1,0:T(4,128)S(1)} %bitcast.4) | data formatting | bytes 65536
where the time goes:
time: 26.3 us; the launch traced here: 26.1 us
  Pallas kernels  25.5 us (97%)
  local copies, waits for them, and re-layouts  0.62 us (2%)
    pallas_call x1, Pallas kernels, per_device(): pl.pallas_call(functools.partial(kernel, n_wide, n_narrow), out_shape=jax...  25.5 us
    unnamed x1, local copies, waits for them, and re-layouts  0.62 us

commit v1 on v0

--- a/solution.py
+++ b/solution.py
@@ -39,11 +39,11 @@
 
 
 def repeat_matrix(n, total, dtype):
-    return (iota((n, total), 0) == lax.rem(iota((n, total), 1), n)).astype(dtype)
+    return (iota((n, total), 0) == (iota((n, total), 1) & (n - 1))).astype(dtype)
 
 
 def band(lane, width, tile, plane, taps):
-    group = lane // width
+    group = lane >> (width.bit_length() - 1)
     first = plane - tile * (128 // width)
     out = jnp.zeros(taps[0].shape, F32)
     for dz in range(3):
@@ -104,6 +104,9 @@
     m_deep,
     m_upward,
     m_decode,
+    m_classes,
+    fine,
+    coarse,
     first,
     skip,
     pooled,
@@ -117,15 +120,22 @@
     w = lax.axis_index("wide")
     n = lax.axis_index("narrow")
 
-    def partner(offset):
-        return (
-            lax.rem(w + offset[0] + n_wide, n_wide),
-            lax.rem(n + offset[1] + n_narrow, n_narrow),
-        )
+    def within(at, count):
+        return jnp.logical_and(at >= 0, at < count)
+
+    def has(dy, dx):
+        return jnp.logical_and(within(w + dy, n_wide), within(n + dx, n_narrow))
+
+    halo[...] = jnp.zeros(halo.shape, BF16)
 
     barrier = pltpu.get_barrier_semaphore()
-    for offset in OFFSETS:
-        pl.semaphore_signal(barrier, inc=1, device_id=partner(offset), device_id_type=MESH)
+    for dy, dx in OFFSETS:
+
+        @pl.when(has(dy, dx))
+        def _():
+            pl.semaphore_signal(
+                barrier, inc=1, device_id=(w + dy, n + dx), device_id_type=MESH
+            )
 
     sources = (
         volume, w_enter, w_encode, w_widen, w_deep, w_upward, w_decode, w_classes,
@@ -154,19 +164,23 @@
     own[...] = by_row
     halo[1, 64:96, :] = by_row
 
-    pl.semaphore_wait(barrier, len(OFFSETS))
-    sends = []
-    for k, offset in enumerate(OFFSETS):
-        send = pltpu.make_async_remote_copy(
+    def exchange(k):
+        dy, dx = OFFSETS[k]
+        return pltpu.make_async_remote_copy(
             src_ref=own,
-            dst_ref=halo.at[1 - offset[1], pl.ds(32 * (2 - offset[0]), 32)],
+            dst_ref=halo.at[1 - dx, pl.ds(32 * (2 - dy), 32)],
             send_sem=send_sem.at[k],
             recv_sem=recv_sem.at[k],
-            device_id=partner(offset),
+            device_id=(w + dy, n + dx),
             device_id_type=MESH,
         )
-        send.start()
-        sends.append(send)
+
+    pl.semaphore_wait(barrier, sum(has(dy, dx).astype(jnp.int32) for dy, dx in OFFSETS))
+    for k, (dy, dx) in enumerate(OFFSETS):
+
+        @pl.when(has(dy, dx))
+        def _():
+            exchange(k).start()
 
     for load in loads[1:]:
         load.wait()
@@ -174,13 +188,13 @@
     def rows_of(refs):
         return jnp.concatenate([ref[...].reshape(1, ref.shape[0]) for ref in refs], axis=0)
 
-    fine = jnp.dot(
+    fine[...] = jnp.dot(
         rows_of((v_gain_enter, v_shift_enter, v_gain_encode, v_shift_encode, v_gain_decode, v_shift_decode)),
         repeat_matrix(32, 256, F32),
         preferred_element_type=F32,
         precision=lax.Precision.HIGHEST,
     )
-    coarse = jnp.dot(
+    coarse[...] = jnp.dot(
         rows_of((v_gain_widen, v_shift_widen, v_gain_deep, v_shift_deep)),
         repeat_matrix(64, 256, F32),
         preferred_element_type=F32,
@@ -188,7 +202,7 @@
     )
 
     taps = dot(v_enter[...], repeat_matrix(32, 256, BF16))
-    offset_of = iota((DEPTH, 256), 0) - iota((DEPTH, 256), 1) // 32 + 1
+    offset_of = iota((DEPTH, 256), 0) - (iota((DEPTH, 256), 1) >> 5) + 1
     zero = jnp.zeros((DEPTH, 256), F32)
     blocks = {}
     for dx in range(3):
@@ -266,7 +280,7 @@
         for z in range(4):
             for tile in range(2):
                 m_upward[tap, 64 * z : 64 * (z + 1), 128 * tile : 128 * (tile + 1)] = jnp.where(
-                    lane64 // 64 == z - 2 * tile, turned, 0.0
+                    (lane64 >> 6) == z - 2 * tile, turned, 0.0
                 ).astype(BF16)
         return carry
 
@@ -280,13 +294,14 @@
         jnp.broadcast_to(classes[0:1], (64, 256)),
         jnp.broadcast_to(classes[1:2], (64, 256)),
     )
-    per_plane = jnp.where(lax.rem(at_row, 32) // 4 == at_lane // 32, per_class, 0.0)
-    m_classes = jnp.concatenate(
-        [jnp.where(lax.rem(at_row, 4) == y, per_plane, 0.0) for y in range(ROWS)], axis=1
-    ).astype(BF16)
+    per_plane = jnp.where(((at_row & 31) >> 2) == (at_lane >> 5), per_class, 0.0)
+    for y in range(ROWS):
+        m_classes[:, 256 * y : 256 * (y + 1)] = jnp.where(
+            (at_row & 3) == y, per_plane, 0.0
+        ).astype(BF16)
 
     def inside(at, count):
-        return jnp.logical_and(at >= 0, at < count).astype(F32)
+        return within(at, count).astype(F32)
 
     left = inside(n - 1, n_narrow)
     right = inside(n + 1, n_narrow)
@@ -310,17 +325,17 @@
         else:
             ref[0, row] = pltpu.roll(value, 1, 0).astype(BF16)
 
-    for send in sends:
-        send.wait()
+    for k, (dy, dx) in enumerate(OFFSETS):
+
+        @pl.when(has(-dy, -dx))
+        def _():
+            exchange(k).wait_recv()
 
     lane = iota((32, 128), 1)
     wide_rows = []
     for block in range(5):
-        keep = inside(w + block - 2, n_wide)
         rows = pl.ds(32 * block, 32)
-        middle = halo[1, rows, :].astype(F32) * keep
-        before = halo[0, rows, :].astype(F32) * (keep * left)
-        after = halo[2, rows, :].astype(F32) * (keep * right)
+        before, middle, after = [halo[side, rows, :].astype(F32) for side in range(3)]
         wide_rows.append(
             jnp.concatenate(
                 [jnp.where(lane < HALF, before, middle), jnp.where(lane < HALF, middle, after)],
@@ -354,7 +369,7 @@
                 keep = inside(w * ROWS - 7 + row, n_wide * ROWS)
                 put_columns(
                     first, row, px,
-                    relu_inside(acc[XC * g : XC * (g + 1)], fine[0:1], fine[1:2], keep),
+                    relu_inside(acc[XC * g : XC * (g + 1)], fine[0:1, :], fine[1:2, :], keep),
                 )
 
     matrix = m_encode[...].reshape(9 * 256, 256)
@@ -366,7 +381,7 @@
             for dx in range(3)
         ]
         parity_acc.append(dot(jnp.concatenate(pieces, axis=1), matrix))
-    pool_lane = lax.rem(iota((XC, 128), 1), 64) < 32
+    pool_lane = (iota((XC, 128), 1) & 32) == 0
     for k in range(8):
         keep = inside(w * 2 - 3 + k, n_wide * 2)
         best = None
@@ -374,7 +389,7 @@
             row = 2 * k + y
             for px in range(2):
                 value = relu_inside(
-                    parity_acc[px][XC * row : XC * (row + 1)], fine[2:3], fine[3:4], keep
+                    parity_acc[px][XC * row : XC * (row + 1)], fine[2:3, :], fine[3:4, :], keep
                 )
                 if 5 <= row <= 10:
                     put_columns(skip, row - 5, px, value)
@@ -394,7 +409,7 @@
     acc = dot(jnp.concatenate(pieces, axis=1), m_widen[...].reshape(9 * 128, 256))
     for k in range(6):
         keep = inside(w * 2 - 2 + k, n_wide * 2)
-        value = relu_inside(acc[XC * k : XC * (k + 1)], coarse[0:1], coarse[1:2], keep)
+        value = relu_inside(acc[XC * k : XC * (k + 1)], coarse[0:1, :], coarse[1:2, :], keep)
         widened[0, k] = pltpu.roll(value, 1, 0).astype(BF16)
         widened[1, k] = value.astype(BF16)
         widened[2, k] = pltpu.roll(value, XC - 1, 0).astype(BF16)
@@ -407,8 +422,8 @@
         [
             relu_inside(
                 acc[XC * k : XC * (k + 1)],
-                coarse[2:3],
-                coarse[3:4],
+                coarse[2:3, :],
+                coarse[3:4, :],
                 inside(w * 2 - 1 + k, n_wide * 2),
             )
             for k in range(4)
@@ -423,7 +438,8 @@
             for k in range(3):
                 put_columns(lifted, 2 * k + 1 - b, e, acc[XC * k : XC * (k + 1)])
 
-    parities = []
+    matrix = m_decode[...].reshape(18 * 256, 256)
+    accs = []
     for px in range(2):
         pieces = [
             ref[px + dx, dy : dy + ROWS, 0:HALF].reshape(ROWS * HALF, 256)
@@ -431,9 +447,9 @@
             for dx in range(3)
             for ref in (skip, lifted)
         ]
-        parities.append(jnp.concatenate(pieces, axis=1))
-    acc = dot(jnp.concatenate(parities, axis=0), m_decode[...].reshape(18 * 256, 256))
-    value = jnp.maximum(acc * fine[4:5] + fine[5:6], 0.0)
+        accs.append(dot(jnp.concatenate(pieces, axis=1), matrix))
+    acc = jnp.concatenate(accs, axis=0)
+    value = jnp.maximum(acc * fine[4:5, :] + fine[5:6, :], 0.0)
     for px in range(2):
         for y in range(ROWS):
             start = (px * ROWS + y) * HALF
@@ -450,7 +466,13 @@
         ],
         axis=1,
     )
-    logits = dot_nt(m_classes, features)
+    logits = dot_nt(m_classes[...], features)
+    for k, (dy, dx) in enumerate(OFFSETS):
+
+        @pl.when(has(dy, dx))
+        def _():
+            exchange(k).wait_send()
+
     out[...] = logits + jnp.where(iota((64, 128), 0) < 32, s_bias[0], s_bias[1])
 
 
@@ -516,6 +538,9 @@
             pltpu.VMEM((9, 256, 256), BF16),
             pltpu.VMEM((4, 256, 256), BF16),
             pltpu.VMEM((9, 2, 256, 256), BF16),
+            pltpu.VMEM((64, 1024), BF16),
+            pltpu.VMEM((6, 256), F32),
+            pltpu.VMEM((4, 256), F32),
             pltpu.VMEM((4, 18, XC, 256), BF16),
             pltpu.VMEM((4, 6, XC, 256), BF16),
             pltpu.VMEM((3, 8, XC, 128), BF16),

time: 26.3 us -> 21.7 us (0.83)
  the two profiles are of different devices: /device:TPU:1 before, /device:TPU:71 now
where the time goes in v1:
time: 21.7 us; the launch traced here: 21.6 us
  Pallas kernels  20.9 us (96%)
  local copies, waits for them, and re-layouts  0.62 us (3%)
    pallas_call x1, Pallas kernels, per_device(): pl.pallas_call(functools.partial(kernel, n_wide, n_narrow), out_shape=jax...  20.9 us
    unnamed x1, local copies, waits for them, and re-layouts  0.62 us

profile of v1, /device:TPU:71, one launch (start us, length us, event | category | flops | bytes accessed | tf_op | source)
XLA Modules:
  0.0 21.6 jit_solution(16646116677645593546)
XLA Ops:
  0.0 20.9 %unet.1 = f32[64,128]{1,0:T(8,128)S(1)} custom-call(bf16[8,4,128]{2,1,0:T(4,128)(2,1)} %bitcast.6, bf16[27,32]{1,0:T(8,128)(2,1)} %bitcast.7, bf16[27,32,32]{2,1,0:T(8,128)(2,1)} %w_encode.1, bf16[27,32,64]{2,1,0:T(8,128)(2,1)} %bitcast.5, bf16[27,64,64]{2,1,0:T(8,128)(2,1)} %w_deep.1, bf16[8,32,64]{2,1,0:T(8,128)(2,1)} %w_upward.1, ...), custom_call_target="tpu_custom_call" | custom-call | tf_op jit(solution)/shard_map/unet/pallas_call | solution.py:525
  20.9 0.6 %copy.21 = f32[2,8,4,128]{3,2,1,0:T(4,128)} copy(f32[2,8,4,128]{3,2,1,0:T(4,128)S(1)} %bitcast.4) | data formatting | bytes 65536

commit v2 on v1

--- a/solution.py
+++ b/solution.py
@@ -19,6 +19,8 @@
 OFFSETS = [
     (dy, dx) for dy in (-2, 2, -1, 1, 0) for dx in (-1, 1, 0) if (dy, dx) != (0, 0)
 ]
+SMALL_LOADS = (1,) + tuple(range(7, 19))
+LARGE_LOADS = tuple(range(2, 7))
 POOL_PLANE = (0, 2, 1, 3)
 
 
@@ -164,26 +166,8 @@
     own[...] = by_row
     halo[1, 64:96, :] = by_row
 
-    def exchange(k):
-        dy, dx = OFFSETS[k]
-        return pltpu.make_async_remote_copy(
-            src_ref=own,
-            dst_ref=halo.at[1 - dx, pl.ds(32 * (2 - dy), 32)],
-            send_sem=send_sem.at[k],
-            recv_sem=recv_sem.at[k],
-            device_id=(w + dy, n + dx),
-            device_id_type=MESH,
-        )
-
-    pl.semaphore_wait(barrier, sum(has(dy, dx).astype(jnp.int32) for dy, dx in OFFSETS))
-    for k, (dy, dx) in enumerate(OFFSETS):
-
-        @pl.when(has(dy, dx))
-        def _():
-            exchange(k).start()
-
-    for load in loads[1:]:
-        load.wait()
+    for k in SMALL_LOADS:
+        loads[k].wait()
 
     def rows_of(refs):
         return jnp.concatenate([ref[...].reshape(1, ref.shape[0]) for ref in refs], axis=0)
@@ -214,67 +198,105 @@
                     offset_of == dz, jnp.broadcast_to(taps[row : row + 1], (DEPTH, 256)), block
                 )
             blocks[dx, dy] = block
-    for yo in range(6):
+    for yo in range(5):
         for px in range(2):
             pieces = [
                 blocks.get((s - px, yin - yo), zero) for s in range(4) for yin in range(8)
             ]
             m_enter[yo, px] = jnp.concatenate(pieces, axis=0).astype(BF16)
 
+    classes = dot(v_classes[...], repeat_matrix(32, 256, BF16))
+    at_row = iota((64, 256), 0)
+    at_lane = iota((64, 256), 1)
+    per_class = jnp.where(
+        at_row < 32,
+        jnp.broadcast_to(classes[0:1], (64, 256)),
+        jnp.broadcast_to(classes[1:2], (64, 256)),
+    )
+    per_plane = jnp.where(((at_row & 31) >> 2) == (at_lane >> 5), per_class, 0.0)
+    for y in range(ROWS):
+        m_classes[:, 256 * y : 256 * (y + 1)] = jnp.where(
+            (at_row & 3) == y, per_plane, 0.0
+        ).astype(BF16)
+
+    def exchange(k):
+        dy, dx = OFFSETS[k]
+        return pltpu.make_async_remote_copy(
+            src_ref=own,
+            dst_ref=halo.at[1 - dx, pl.ds(32 * (2 - dy), 32)],
+            send_sem=send_sem.at[k],
+            recv_sem=recv_sem.at[k],
+            device_id=(w + dy, n + dx),
+            device_id_type=MESH,
+        )
+
+    pl.semaphore_wait(barrier, sum(has(dy, dx).astype(jnp.int32) for dy, dx in OFFSETS))
+    for k, (dy, dx) in enumerate(OFFSETS):
+
+        @pl.when(has(dy, dx))
+        def _():
+            exchange(k).start()
+
+    for k in LARGE_LOADS:
+        loads[k].wait()
+
     eye32 = eye(32)
     eye64 = eye(64)
+    repeat64 = repeat_matrix(64, 128, BF16)
     lane32 = iota((32, 128), 1)
     lane64 = iota((64, 128), 1)
 
-    def build_fine(tap, carry):
-        rows = [v_encode[9 * dz + tap] for dz in range(3) for _ in range(4)]
-        turned = dot_nt(eye32, jnp.concatenate(rows, axis=0))
-        parts = [turned[:, 128 * dz : 128 * (dz + 1)] for dz in range(3)]
-        for z in range(DEPTH):
-            for tile in range(2):
-                m_encode[tap, 32 * z : 32 * (z + 1), 128 * tile : 128 * (tile + 1)] = band(
-                    lane32, 32, tile, z, parts
-                ).astype(BF16)
-        rows = [v_decode[9 * dz + tap] for dz in range(3) for _ in range(4)]
-        turned = dot_nt(eye64, jnp.concatenate(rows, axis=0))
-        for source in range(2):
-            parts = [
-                turned[32 * source : 32 * (source + 1), 128 * dz : 128 * (dz + 1)]
-                for dz in range(3)
-            ]
+    def build_fine(dy, carry):
+        for dx in range(3):
+            tap = 3 * dy + dx
+            rows = [v_encode[9 * dz + tap] for dz in range(3) for _ in range(4)]
+            turned = dot_nt(eye32, jnp.concatenate(rows, axis=0))
+            parts = [turned[:, 128 * dz : 128 * (dz + 1)] for dz in range(3)]
             for z in range(DEPTH):
                 for tile in range(2):
-                    m_decode[
-                        tap, source, 32 * z : 32 * (z + 1), 128 * tile : 128 * (tile + 1)
-                    ] = band(lane32, 32, tile, z, parts).astype(BF16)
+                    m_encode[tap, 32 * z : 32 * (z + 1), 128 * tile : 128 * (tile + 1)] = band(
+                        lane32, 32, tile, z, parts
+                    ).astype(BF16)
+            rows = [v_decode[9 * dz + tap] for dz in range(3) for _ in range(4)]
+            turned = dot_nt(eye64, jnp.concatenate(rows, axis=0))
+            for source in range(2):
+                parts = [
+                    turned[32 * source : 32 * (source + 1), 128 * dz : 128 * (dz + 1)]
+                    for dz in range(3)
+                ]
+                for z in range(DEPTH):
+                    for tile in range(2):
+                        m_decode[
+                            source, tap, 32 * z : 32 * (z + 1), 128 * tile : 128 * (tile + 1)
+                        ] = band(lane32, 32, tile, z, parts).astype(BF16)
         return carry
 
-    lax.fori_loop(0, 9, build_fine, 0)
-
-    repeat64 = repeat_matrix(64, 128, BF16)
-
-    def build_coarse(tap, carry):
-        rows = [v_widen[9 * dz + tap] for dz in range(3)]
-        turned = dot(jnp.concatenate(rows, axis=0), repeat64)
-        parts = [turned[32 * dz : 32 * (dz + 1)] for dz in range(3)]
-        for group in range(4):
-            for tile in range(2):
-                m_widen[tap, 32 * group : 32 * (group + 1), 128 * tile : 128 * (tile + 1)] = band(
-                    lane32, 64, tile, POOL_PLANE[group], parts
-                ).astype(BF16)
-        rows = [v_deep[9 * dz + tap] for dz in range(3) for _ in range(2)]
-        turned = dot_nt(eye64, jnp.concatenate(rows, axis=0))
-        parts = [turned[:, 128 * dz : 128 * (dz + 1)] for dz in range(3)]
-        for z in range(4):
-            for tile in range(2):
-                m_deep[tap, 64 * z : 64 * (z + 1), 128 * tile : 128 * (tile + 1)] = band(
-                    lane64, 64, tile, z, parts
-                ).astype(BF16)
+    lax.fori_loop(0, 3, build_fine, 0)
+
+    def build_coarse(dy, carry):
+        for dx in range(3):
+            tap = 3 * dy + dx
+            rows = [v_widen[9 * dz + tap] for dz in range(3)]
+            turned = dot(jnp.concatenate(rows, axis=0), repeat64)
+            parts = [turned[32 * dz : 32 * (dz + 1)] for dz in range(3)]
+            for group in range(4):
+                for tile in range(2):
+                    m_widen[
+                        tap, 32 * group : 32 * (group + 1), 128 * tile : 128 * (tile + 1)
+                    ] = band(lane32, 64, tile, POOL_PLANE[group], parts).astype(BF16)
+            rows = [v_deep[9 * dz + tap] for dz in range(3) for _ in range(2)]
+            turned = dot_nt(eye64, jnp.concatenate(rows, axis=0))
+            parts = [turned[:, 128 * dz : 128 * (dz + 1)] for dz in range(3)]
+            for z in range(4):
+                for tile in range(2):
+                    m_deep[tap, 64 * z : 64 * (z + 1), 128 * tile : 128 * (tile + 1)] = band(
+                        lane64, 64, tile, z, parts
+                    ).astype(BF16)
         return carry
 
-    lax.fori_loop(0, 9, build_coarse, 0)
-
-    def build_upward(tap, carry):
+    lax.fori_loop(0, 3, build_coarse, 0)
+
+    for tap in range(4):
         rows = [v_upward[4 * a + tap] for _ in range(2) for a in range(2)]
         turned = dot_nt(eye64, jnp.concatenate(rows, axis=0))
         for z in range(4):
@@ -282,23 +304,6 @@
                 m_upward[tap, 64 * z : 64 * (z + 1), 128 * tile : 128 * (tile + 1)] = jnp.where(
                     (lane64 >> 6) == z - 2 * tile, turned, 0.0
                 ).astype(BF16)
-        return carry
-
-    lax.fori_loop(0, 4, build_upward, 0)
-
-    classes = dot(v_classes[...], repeat_matrix(32, 256, BF16))
-    at_row = iota((64, 256), 0)
-    at_lane = iota((64, 256), 1)
-    per_class = jnp.where(
-        at_row < 32,
-        jnp.broadcast_to(classes[0:1], (64, 256)),
-        jnp.broadcast_to(classes[1:2], (64, 256)),
-    )
-    per_plane = jnp.where(((at_row & 31) >> 2) == (at_lane >> 5), per_class, 0.0)
-    for y in range(ROWS):
-        m_classes[:, 256 * y : 256 * (y + 1)] = jnp.where(
-            (at_row & 3) == y, per_plane, 0.0
-        ).astype(BF16)
 
     def inside(at, count):
         return within(at, count).astype(F32)
@@ -319,94 +324,118 @@
         )
 
     def put_columns(ref, row, parity, value):
-        ref[1 + parity, row] = value.astype(BF16)
+        ref[(1 + parity, *row)] = value.astype(BF16)
         if parity == 0:
-            ref[3, row] = pltpu.roll(value, XC - 1, 0).astype(BF16)
+            ref[(3, *row)] = pltpu.roll(value, XC - 1, 0).astype(BF16)
         else:
-            ref[0, row] = pltpu.roll(value, 1, 0).astype(BF16)
-
-    for k, (dy, dx) in enumerate(OFFSETS):
-
-        @pl.when(has(-dy, -dx))
-        def _():
-            exchange(k).wait_recv()
-
-    lane = iota((32, 128), 1)
-    wide_rows = []
-    for block in range(5):
-        rows = pl.ds(32 * block, 32)
-        before, middle, after = [halo[side, rows, :].astype(F32) for side in range(3)]
-        wide_rows.append(
-            jnp.concatenate(
-                [jnp.where(lane < HALF, before, middle), jnp.where(lane < HALF, middle, after)],
-                axis=1,
-            )
-        )
-    wide_rows = jnp.concatenate(wide_rows, axis=0)
-    shifted = [
-        (wide_rows if s == 1 else pltpu.roll(wide_rows, (1 - s) % 256, 1)).astype(BF16)
-        for s in range(4)
-    ]
+            ref[(0, *row)] = pltpu.roll(value, 1, 0).astype(BF16)
+
+    lane = iota((96, 128), 1)
     at = iota((XC, 256), 0)
     pick = (
         iota((XC, 256), 1) == 2 * jnp.where(at < 72, at, at - XC) + HALF
     ).astype(BF16)
-    columns = jnp.concatenate(
-        [
-            dot_nt(
-                pick, jnp.concatenate([piece[48 * g : 48 * g + 64] for piece in shifted], axis=0)
-            ).astype(BF16)
-            for g in range(3)
-        ],
-        axis=0,
-    )
-
-    for yo in range(6):
+    pool_lane = (iota((XC, 128), 1) & 32) == 0
+    encode_matrix = m_encode[...].reshape(9 * 256, 256)
+    near = jnp.where(lax.rem(w, 4) < 2, 1, 0)
+
+    for turn in range(2):
+        half = near if turn == 0 else 1 - near
+        for k, (dy, dx) in enumerate(OFFSETS):
+            first_half = 1 if dy < 0 else 0
+            if dy == 0:
+                now = turn == 0
+            else:
+                now = near == first_half if turn == 0 else near != first_half
+
+            @pl.when(jnp.logical_and(has(-dy, -dx), now))
+            def _():
+                exchange(k).wait_recv()
+
+        rows = pl.ds(pl.multiple_of(64 * half, 64), 96)
+        before, middle, after = [halo[side, rows, :].astype(F32) for side in range(3)]
+        wide_rows = jnp.concatenate(
+            [jnp.where(lane < HALF, before, middle), jnp.where(lane < HALF, middle, after)],
+            axis=1,
+        )
+        wide_rows = jnp.concatenate([wide_rows, jnp.zeros((8, 256), F32)], axis=0)
+        shifted = [
+            wide_rows if s == 1 else pltpu.roll(wide_rows, (1 - s) % 256, 1) for s in range(4)
+        ]
+        columns = jnp.concatenate(
+            [
+                dot_nt(
+                    pick,
+                    jnp.concatenate(
+                        [piece[40 * g : 40 * g + 64] for piece in shifted], axis=0
+                    ).astype(BF16),
+                ).astype(BF16)
+                for g in range(2)
+            ],
+            axis=0,
+        )
+
+        for yo in range(5):
+            for px in range(2):
+                acc = dot(columns, m_enter[yo, px])
+                for g in range(2):
+                    row = 5 * g + yo
+                    keep = inside(w * ROWS - 7 + 8 * half + row, n_wide * ROWS)
+                    put_columns(
+                        first, (turn, row), px,
+                        relu_inside(
+                            acc[XC * g : XC * (g + 1)], fine[0:1, :], fine[1:2, :], keep
+                        ),
+                    )
+
+        parity_acc = []
         for px in range(2):
-            acc = dot(columns, m_enter[yo, px])
-            for g in range(3):
-                row = 6 * g + yo
-                keep = inside(w * ROWS - 7 + row, n_wide * ROWS)
-                put_columns(
-                    first, row, px,
-                    relu_inside(acc[XC * g : XC * (g + 1)], fine[0:1, :], fine[1:2, :], keep),
-                )
-
-    matrix = m_encode[...].reshape(9 * 256, 256)
-    parity_acc = []
-    for px in range(2):
+            pieces = [
+                first[px + dx, turn, dy : dy + 8].reshape(8 * XC, 256)
+                for dy in range(3)
+                for dx in range(3)
+            ]
+            parity_acc.append(dot(jnp.concatenate(pieces, axis=1), encode_matrix))
+        for k in range(4):
+            keep = inside(w * 2 - 3 + 4 * half + k, n_wide * 2)
+            best = None
+            for y in range(2):
+                row = 2 * k + y
+                for px in range(2):
+                    value = relu_inside(
+                        parity_acc[px][XC * row : XC * (row + 1)],
+                        fine[2:3, :], fine[3:4, :], keep,
+                    )
+                    if row not in (3, 4):
+                        put_columns(skip, (8 * half + row,), px, value)
+                    best = value if best is None else jnp.maximum(best, value)
+            low = best[:, 0:128]
+            high = best[:, 128:256]
+            low = jnp.maximum(low, pltpu.roll(low, 96, 1))
+            high = jnp.maximum(high, pltpu.roll(high, 96, 1))
+            best = jnp.where(pool_lane, low, pltpu.roll(high, 32, 1))
+            pooled[0, 4 * half + k] = pltpu.roll(best, 1, 0).astype(BF16)
+            pooled[1, 4 * half + k] = best.astype(BF16)
+            pooled[2, 4 * half + k] = pltpu.roll(best, XC - 1, 0).astype(BF16)
+
+    def decode_part(px, source):
+        ref, start = ((skip, 5), (lifted, 0))[source]
         pieces = [
-            first[px + dx, dy : dy + 16].reshape(16 * XC, 256)
+            ref[px + dx, start + dy : start + dy + ROWS, 0:HALF].reshape(ROWS * HALF, 256)
             for dy in range(3)
             for dx in range(3)
         ]
-        parity_acc.append(dot(jnp.concatenate(pieces, axis=1), matrix))
-    pool_lane = (iota((XC, 128), 1) & 32) == 0
-    for k in range(8):
-        keep = inside(w * 2 - 3 + k, n_wide * 2)
-        best = None
-        for y in range(2):
-            row = 2 * k + y
-            for px in range(2):
-                value = relu_inside(
-                    parity_acc[px][XC * row : XC * (row + 1)], fine[2:3, :], fine[3:4, :], keep
-                )
-                if 5 <= row <= 10:
-                    put_columns(skip, row - 5, px, value)
-                best = value if best is None else jnp.maximum(best, value)
-        low = best[:, 0:128]
-        high = best[:, 128:256]
-        low = jnp.maximum(low, pltpu.roll(low, 96, 1))
-        high = jnp.maximum(high, pltpu.roll(high, 96, 1))
-        best = jnp.where(pool_lane, low, pltpu.roll(high, 32, 1))
-        pooled[0, k] = pltpu.roll(best, 1, 0).astype(BF16)
-        pooled[1, k] = best.astype(BF16)
-        pooled[2, k] = pltpu.roll(best, XC - 1, 0).astype(BF16)
+        return dot(
+            jnp.concatenate(pieces, axis=1), m_decode[source].reshape(9 * 256, 256)
+        )
+
+    from_skip = [decode_part(0, 0)]
 
     pieces = [
         pooled[dx, dy : dy + 6].reshape(6 * XC, 128) for dy in range(3) for dx in range(3)
     ]
     acc = dot(jnp.concatenate(pieces, axis=1), m_widen[...].reshape(9 * 128, 256))
+    from_skip.append(decode_part(1, 0))
     for k in range(6):
         keep = inside(w * 2 - 2 + k, n_wide * 2)
         value = relu_inside(acc[XC * k : XC * (k + 1)], coarse[0:1, :], coarse[1:2, :], keep)
@@ -436,19 +465,9 @@
         for e in range(2):
             acc = dot(source, m_upward[2 * b + e])
             for k in range(3):
-                put_columns(lifted, 2 * k + 1 - b, e, acc[XC * k : XC * (k + 1)])
-
-    matrix = m_decode[...].reshape(18 * 256, 256)
-    accs = []
-    for px in range(2):
-        pieces = [
-            ref[px + dx, dy : dy + ROWS, 0:HALF].reshape(ROWS * HALF, 256)
-            for dy in range(3)
-            for dx in range(3)
-            for ref in (skip, lifted)
-        ]
-        accs.append(dot(jnp.concatenate(pieces, axis=1), matrix))
-    acc = jnp.concatenate(accs, axis=0)
+                put_columns(lifted, (2 * k + 1 - b,), e, acc[XC * k : XC * (k + 1)])
+
+    acc = jnp.concatenate([from_skip[px] + decode_part(px, 1) for px in range(2)], axis=0)
     value = jnp.maximum(acc * fine[4:5, :] + fine[5:6, :], 0.0)
     for px in range(2):
         for y in range(ROWS):
@@ -532,17 +551,17 @@
             pltpu.VMEM((32, COLS), F32),
             pltpu.VMEM((32, COLS), BF16),
             pltpu.VMEM((3, 160, COLS), BF16),
-            pltpu.VMEM((6, 2, 256, 256), BF16),
+            pltpu.VMEM((5, 2, 256, 256), BF16),
             pltpu.VMEM((9, 256, 256), BF16),
             pltpu.VMEM((9, 128, 256), BF16),
             pltpu.VMEM((9, 256, 256), BF16),
             pltpu.VMEM((4, 256, 256), BF16),
-            pltpu.VMEM((9, 2, 256, 256), BF16),
+            pltpu.VMEM((2, 9, 256, 256), BF16),
             pltpu.VMEM((64, 1024), BF16),
             pltpu.VMEM((6, 256), F32),
             pltpu.VMEM((4, 256), F32),
-            pltpu.VMEM((4, 18, XC, 256), BF16),
-            pltpu.VMEM((4, 6, XC, 256), BF16),
+            pltpu.VMEM((4, 2, 10, XC, 256), BF16),
+            pltpu.VMEM((4, 16, XC, 256), BF16),
             pltpu.VMEM((3, 8, XC, 128), BF16),
             pltpu.VMEM((3, 6, XC, 256), BF16),
             pltpu.VMEM((4, 6, XC, 256), BF16),

time: 21.7 us -> 20.4 us (0.940)
  Pallas kernels: 20.9 us -> 19.7 us
    pallas_call x1, Pallas kernels: 20.9 us -> 19.7 us  [per_device(): pl.pallas_call(functools.partial(kernel, n_wide, n_narrow), out_shape=jax...]
where the time goes in v2:
time: 20.4 us; the launch traced here: 20.3 us
  Pallas kernels  19.7 us (97%)
  local copies, waits for them, and re-layouts  0.62 us (3%)
    pallas_call x1, Pallas kernels, per_device(): pl.pallas_call(functools.partial(kernel, n_wide, n_narrow), out_shape=jax...  19.7 us
    unnamed x1, local copies, waits for them, and re-layouts  0.62 us

profile of v2, /device:TPU:71, one launch (start us, length us, event | category | flops | bytes accessed | tf_op | source)
XLA Modules:
  0.0 20.3 jit_solution(4994925495752238704)
XLA Ops:
  0.0 19.7 %unet.1 = f32[64,128]{1,0:T(8,128)S(1)} custom-call(bf16[8,4,128]{2,1,0:T(4,128)(2,1)} %bitcast.6, bf16[27,32]{1,0:T(8,128)(2,1)} %bitcast.7, bf16[27,32,32]{2,1,0:T(8,128)(2,1)} %w_encode.1, bf16[27,32,64]{2,1,0:T(8,128)(2,1)} %bitcast.5, bf16[27,64,64]{2,1,0:T(8,128)(2,1)} %w_deep.1, bf16[8,32,64]{2,1,0:T(8,128)(2,1)} %w_upward.1, ...), custom_call_target="tpu_custom_call" | custom-call | tf_op jit(solution)/shard_map/unet/pallas_call | solution.py:544
  19.7 0.6 %copy.21 = f32[2,8,4,128]{3,2,1,0:T(4,128)} copy(f32[2,8,4,128]{3,2,1,0:T(4,128)S(1)} %bitcast.4) | data formatting | bytes 65536

commit v3 on v2

--- a/solution.py
+++ b/solution.py
@@ -44,15 +44,18 @@
     return (iota((n, total), 0) == (iota((n, total), 1) & (n - 1))).astype(dtype)
 
 
-def band(lane, width, tile, plane, taps):
-    group = lane >> (width.bit_length() - 1)
-    first = plane - tile * (128 // width)
-    out = jnp.zeros(taps[0].shape, F32)
-    for dz in range(3):
-        place = first + 1 - dz
-        if 0 <= place < 128 // width:
-            out = jnp.where(group == place, taps[dz], out)
-    return out
+def bands(width, taps):
+    count = 128 // width
+    lane = iota(taps[0].shape, 1)
+    places = [((lane >> (width.bit_length() - 1)) == p).astype(BF16) for p in range(count)]
+    placed = [[tap.astype(BF16) * place for place in places] for tap in taps]
+    blocks = {}
+    for first in range(-1, count + 1):
+        terms = [
+            placed[dz][first + 1 - dz] for dz in range(3) if 0 <= first + 1 - dz < count
+        ]
+        blocks[first] = functools.reduce(jnp.add, terms)
+    return blocks
 
 
 def kernel(
@@ -166,6 +169,24 @@
     own[...] = by_row
     halo[1, 64:96, :] = by_row
 
+    def exchange(k):
+        dy, dx = OFFSETS[k]
+        return pltpu.make_async_remote_copy(
+            src_ref=own,
+            dst_ref=halo.at[1 - dx, pl.ds(32 * (2 - dy), 32)],
+            send_sem=send_sem.at[k],
+            recv_sem=recv_sem.at[k],
+            device_id=(w + dy, n + dx),
+            device_id_type=MESH,
+        )
+
+    pl.semaphore_wait(barrier, sum(has(dy, dx).astype(jnp.int32) for dy, dx in OFFSETS))
+    for k, (dy, dx) in enumerate(OFFSETS):
+
+        @pl.when(has(dy, dx))
+        def _():
+            exchange(k).start()
+
     for k in SMALL_LOADS:
         loads[k].wait()
 
@@ -219,91 +240,79 @@
             (at_row & 3) == y, per_plane, 0.0
         ).astype(BF16)
 
-    def exchange(k):
-        dy, dx = OFFSETS[k]
-        return pltpu.make_async_remote_copy(
-            src_ref=own,
-            dst_ref=halo.at[1 - dx, pl.ds(32 * (2 - dy), 32)],
-            send_sem=send_sem.at[k],
-            recv_sem=recv_sem.at[k],
-            device_id=(w + dy, n + dx),
-            device_id_type=MESH,
-        )
-
-    pl.semaphore_wait(barrier, sum(has(dy, dx).astype(jnp.int32) for dy, dx in OFFSETS))
-    for k, (dy, dx) in enumerate(OFFSETS):
-
-        @pl.when(has(dy, dx))
-        def _():
-            exchange(k).start()
-
     for k in LARGE_LOADS:
         loads[k].wait()
 
-    eye32 = eye(32)
-    eye64 = eye(64)
     repeat64 = repeat_matrix(64, 128, BF16)
-    lane32 = iota((32, 128), 1)
     lane64 = iota((64, 128), 1)
-
-    def build_fine(dy, carry):
-        for dx in range(3):
-            tap = 3 * dy + dx
-            rows = [v_encode[9 * dz + tap] for dz in range(3) for _ in range(4)]
-            turned = dot_nt(eye32, jnp.concatenate(rows, axis=0))
-            parts = [turned[:, 128 * dz : 128 * (dz + 1)] for dz in range(3)]
+    zero32 = jnp.zeros((32, 128), BF16)
+    zero64 = jnp.zeros((64, 128), BF16)
+
+    eye256 = eye(256)
+
+    def turn_taps(ref):
+        channels = ref.shape[2]
+        count = 256 // channels
+        turned = []
+        for start in range(0, 27, count):
+            row = jnp.concatenate(
+                [ref[min(start + k, 26)] for k in range(count)], axis=1
+            )
+            result = dot_nt(
+                eye256, jnp.concatenate([row] * (128 // ref.shape[1]), axis=0)
+            ).astype(BF16)
+            turned += [result[channels * k : channels * (k + 1)] for k in range(count)]
+        return turned
+
+    from_encode = turn_taps(v_encode)
+    from_decode = turn_taps(v_decode)
+    for tap in range(9):
+        blocks = bands(32, [from_encode[9 * dz + tap] for dz in range(3)])
+        for z in range(DEPTH):
+            for tile in range(2):
+                m_encode[tap, 32 * z : 32 * (z + 1), 128 * tile : 128 * (tile + 1)] = (
+                    blocks.get(z - 4 * tile, zero32)
+                )
+        for source in range(2):
+            blocks = bands(
+                32,
+                [from_decode[9 * dz + tap][32 * source : 32 * (source + 1)] for dz in range(3)],
+            )
             for z in range(DEPTH):
                 for tile in range(2):
-                    m_encode[tap, 32 * z : 32 * (z + 1), 128 * tile : 128 * (tile + 1)] = band(
-                        lane32, 32, tile, z, parts
-                    ).astype(BF16)
-            rows = [v_decode[9 * dz + tap] for dz in range(3) for _ in range(4)]
-            turned = dot_nt(eye64, jnp.concatenate(rows, axis=0))
-            for source in range(2):
-                parts = [
-                    turned[32 * source : 32 * (source + 1), 128 * dz : 128 * (dz + 1)]
-                    for dz in range(3)
-                ]
-                for z in range(DEPTH):
-                    for tile in range(2):
-                        m_decode[
-                            source, tap, 32 * z : 32 * (z + 1), 128 * tile : 128 * (tile + 1)
-                        ] = band(lane32, 32, tile, z, parts).astype(BF16)
-        return carry
-
-    lax.fori_loop(0, 3, build_fine, 0)
-
-    def build_coarse(dy, carry):
-        for dx in range(3):
-            tap = 3 * dy + dx
-            rows = [v_widen[9 * dz + tap] for dz in range(3)]
-            turned = dot(jnp.concatenate(rows, axis=0), repeat64)
-            parts = [turned[32 * dz : 32 * (dz + 1)] for dz in range(3)]
-            for group in range(4):
-                for tile in range(2):
-                    m_widen[
-                        tap, 32 * group : 32 * (group + 1), 128 * tile : 128 * (tile + 1)
-                    ] = band(lane32, 64, tile, POOL_PLANE[group], parts).astype(BF16)
-            rows = [v_deep[9 * dz + tap] for dz in range(3) for _ in range(2)]
-            turned = dot_nt(eye64, jnp.concatenate(rows, axis=0))
-            parts = [turned[:, 128 * dz : 128 * (dz + 1)] for dz in range(3)]
-            for z in range(4):
-                for tile in range(2):
-                    m_deep[tap, 64 * z : 64 * (z + 1), 128 * tile : 128 * (tile + 1)] = band(
-                        lane64, 64, tile, z, parts
-                    ).astype(BF16)
-        return carry
-
-    lax.fori_loop(0, 3, build_coarse, 0)
-
-    for tap in range(4):
-        rows = [v_upward[4 * a + tap] for _ in range(2) for a in range(2)]
-        turned = dot_nt(eye64, jnp.concatenate(rows, axis=0))
+                    m_decode[
+                        source, tap, 32 * z : 32 * (z + 1), 128 * tile : 128 * (tile + 1)
+                    ] = blocks.get(z - 4 * tile, zero32)
+
+    from_widen = dot(v_widen[...].reshape(27 * 32, 64), repeat64).astype(BF16)
+    from_deep = turn_taps(v_deep)
+    for tap in range(9):
+        starts = [32 * (9 * dz + tap) for dz in range(3)]
+        blocks = bands(64, [from_widen[start : start + 32] for start in starts])
+        for group in range(4):
+            for tile in range(2):
+                m_widen[
+                    tap, 32 * group : 32 * (group + 1), 128 * tile : 128 * (tile + 1)
+                ] = blocks.get(POOL_PLANE[group] - 2 * tile, zero32)
+        blocks = bands(64, [from_deep[9 * dz + tap] for dz in range(3)])
         for z in range(4):
             for tile in range(2):
-                m_upward[tap, 64 * z : 64 * (z + 1), 128 * tile : 128 * (tile + 1)] = jnp.where(
-                    (lane64 >> 6) == z - 2 * tile, turned, 0.0
-                ).astype(BF16)
+                m_deep[tap, 64 * z : 64 * (z + 1), 128 * tile : 128 * (tile + 1)] = (
+                    blocks.get(z - 2 * tile, zero64)
+                )
+
+    rows = [
+        jnp.concatenate([v_upward[4 * a + tap] for tap in range(4)], axis=1) for a in range(2)
+    ]
+    turned = dot_nt(eye256, jnp.concatenate(rows + rows, axis=0)).astype(BF16)
+    halves = [((lane64 >> 6) == half).astype(BF16) for half in range(2)]
+    for tap in range(4):
+        block = turned[64 * tap : 64 * (tap + 1)]
+        for z in range(4):
+            for tile in range(2):
+                m_upward[tap, 64 * z : 64 * (z + 1), 128 * tile : 128 * (tile + 1)] = (
+                    block * halves[z - 2 * tile] if 0 <= z - 2 * tile < 2 else zero64
+                )
 
     def inside(at, count):
         return within(at, count).astype(F32)

time: 20.4 us -> 20.5 us (level)
  no operation moved by 1% of the time
where the time goes in v3:
time: 20.5 us; the launch traced here: 20.3 us
  Pallas kernels  19.7 us (96%)
  local copies, waits for them, and re-layouts  0.62 us (3%)
    pallas_call x1, Pallas kernels, per_device(): pl.pallas_call(functools.partial(kernel, n_wide, n_narrow), out_shape=jax...  19.7 us
    unnamed x1, local copies, waits for them, and re-layouts  0.62 us

profile of v3, /device:TPU:71, one launch (start us, length us, event | category | flops | bytes accessed | tf_op | source)
XLA Modules:
  0.0 20.3 jit_solution(2695036881147610599)
XLA Ops:
  0.0 19.7 %unet.1 = f32[64,128]{1,0:T(8,128)S(1)} custom-call(bf16[8,4,128]{2,1,0:T(4,128)(2,1)} %bitcast.6, bf16[27,32]{1,0:T(8,128)(2,1)} %bitcast.7, bf16[27,32,32]{2,1,0:T(8,128)(2,1)} %w_encode.1, bf16[27,32,64]{2,1,0:T(8,128)(2,1)} %bitcast.5, bf16[27,64,64]{2,1,0:T(8,128)(2,1)} %w_deep.1, bf16[8,32,64]{2,1,0:T(8,128)(2,1)} %w_upward.1, ...), custom_call_target="tpu_custom_call" | custom-call | tf_op jit(solution)/shard_map/unet/pallas_call | solution.py:553
  19.7 0.6 %copy.21 = f32[2,8,4,128]{3,2,1,0:T(4,128)} copy(f32[2,8,4,128]{3,2,1,0:T(4,128)S(1)} %bitcast.4) | data formatting | bytes 65536

commit v4 on v3

--- a/solution.py
+++ b/solution.py
@@ -427,24 +427,10 @@
             pooled[1, 4 * half + k] = best.astype(BF16)
             pooled[2, 4 * half + k] = pltpu.roll(best, XC - 1, 0).astype(BF16)
 
-    def decode_part(px, source):
-        ref, start = ((skip, 5), (lifted, 0))[source]
-        pieces = [
-            ref[px + dx, start + dy : start + dy + ROWS, 0:HALF].reshape(ROWS * HALF, 256)
-            for dy in range(3)
-            for dx in range(3)
-        ]
-        return dot(
-            jnp.concatenate(pieces, axis=1), m_decode[source].reshape(9 * 256, 256)
-        )
-
-    from_skip = [decode_part(0, 0)]
-
     pieces = [
         pooled[dx, dy : dy + 6].reshape(6 * XC, 128) for dy in range(3) for dx in range(3)
     ]
     acc = dot(jnp.concatenate(pieces, axis=1), m_widen[...].reshape(9 * 128, 256))
-    from_skip.append(decode_part(1, 0))
     for k in range(6):
         keep = inside(w * 2 - 2 + k, n_wide * 2)
         value = relu_inside(acc[XC * k : XC * (k + 1)], coarse[0:1, :], coarse[1:2, :], keep)
@@ -476,7 +462,16 @@
             for k in range(3):
                 put_columns(lifted, (2 * k + 1 - b,), e, acc[XC * k : XC * (k + 1)])
 
-    acc = jnp.concatenate([from_skip[px] + decode_part(px, 1) for px in range(2)], axis=0)
+    accs = []
+    for px in range(2):
+        pieces = [
+            ref[px + dx, start + dy : start + dy + ROWS, 0:HALF].reshape(ROWS * HALF, 256)
+            for ref, start in ((skip, 5), (lifted, 0))
+            for dy in range(3)
+            for dx in range(3)
+        ]
+        accs.append(dot(jnp.concatenate(pieces, axis=1), m_decode[...].reshape(18 * 256, 256)))
+    acc = jnp.concatenate(accs, axis=0)
     value = jnp.maximum(acc * fine[4:5, :] + fine[5:6, :], 0.0)
     for px in range(2):
         for y in range(ROWS):

time: 20.5 us -> 20.4 us (level)
  no operation moved by 1% of the time
where the time goes in v4:
time: 20.4 us; the launch traced here: 20.3 us
  Pallas kernels  19.7 us (97%)
  local copies, waits for them, and re-layouts  0.62 us (3%)
    pallas_call x1, Pallas kernels, per_device(): pl.pallas_call(functools.partial(kernel, n_wide, n_narrow), out_shape=jax...  19.7 us
    unnamed x1, local copies, waits for them, and re-layouts  0.62 us

profile of v4, /device:TPU:71, one launch (start us, length us, event | category | flops | bytes accessed | tf_op | source)
XLA Modules:
  0.0 20.3 jit_solution(569896479562350076)
XLA Ops:
  0.0 19.7 %unet.1 = f32[64,128]{1,0:T(8,128)S(1)} custom-call(bf16[8,4,128]{2,1,0:T(4,128)(2,1)} %bitcast.6, bf16[27,32]{1,0:T(8,128)(2,1)} %bitcast.7, bf16[27,32,32]{2,1,0:T(8,128)(2,1)} %w_encode.1, bf16[27,32,64]{2,1,0:T(8,128)(2,1)} %bitcast.5, bf16[27,64,64]{2,1,0:T(8,128)(2,1)} %w_deep.1, bf16[8,32,64]{2,1,0:T(8,128)(2,1)} %w_upward.1, ...), custom_call_target="tpu_custom_call" | custom-call | tf_op jit(solution)/shard_map/unet/pallas_call | solution.py:548
  19.7 0.6 %copy.21 = f32[2,8,4,128]{3,2,1,0:T(4,128)} copy(f32[2,8,4,128]{3,2,1,0:T(4,128)S(1)} %bitcast.4) | data formatting | bytes 65536

commit v5 on v4

--- a/solution.py
+++ b/solution.py
@@ -102,7 +102,9 @@
     s_bias,
     plane_rows,
     own,
+    own_edge,
     halo,
+    edges,
     m_enter,
     m_encode,
     m_widen,
@@ -132,6 +134,7 @@
         return jnp.logical_and(within(w + dy, n_wide), within(n + dx, n_narrow))
 
     halo[...] = jnp.zeros(halo.shape, BF16)
+    edges[...] = jnp.zeros(edges.shape, BF16)
 
     barrier = pltpu.get_barrier_semaphore()
     for dy, dx in OFFSETS:
@@ -165,15 +168,22 @@
     by_row = jnp.concatenate(
         [plane_rows[pl.ds(y, DEPTH, stride=ROWS), :] for y in range(ROWS)], axis=0
     )
-    by_row = pltpu.roll(by_row, HALF, 1).astype(BF16)
-    own[...] = by_row
-    halo[1, 64:96, :] = by_row
+    by_row = pltpu.roll(by_row, HALF, 1)
+    own[...] = by_row.astype(BF16)
+    halo[64:96, :] = by_row.astype(BF16)
+    own_edge[...] = jnp.where(
+        iota((16, COLS), 1) < 80, by_row[0:16], pltpu.roll(by_row[16:32], 32, 1)
+    ).astype(BF16)
 
     def exchange(k):
         dy, dx = OFFSETS[k]
+        if dx == 0:
+            source, target = own, halo.at[pl.ds(32 * (2 - dy), 32)]
+        else:
+            source, target = own_edge, edges.at[(1 - dx) // 2, pl.ds(16 * (2 - dy), 16)]
         return pltpu.make_async_remote_copy(
-            src_ref=own,
-            dst_ref=halo.at[1 - dx, pl.ds(32 * (2 - dy), 32)],
+            src_ref=source,
+            dst_ref=target,
             send_sem=send_sem.at[k],
             recv_sem=recv_sem.at[k],
             device_id=(w + dy, n + dx),
@@ -362,7 +372,17 @@
                 exchange(k).wait_recv()
 
         rows = pl.ds(pl.multiple_of(64 * half, 64), 96)
-        before, middle, after = [halo[side, rows, :].astype(F32) for side in range(3)]
+        middle = halo[rows, :].astype(F32)
+        rows = pl.ds(pl.multiple_of(32 * half, 32), 48)
+        sides = []
+        for side in range(2):
+            packed = edges[side, rows, :].astype(F32)
+            pieces = []
+            for block in range(3):
+                piece = packed[16 * block : 16 * (block + 1)]
+                pieces += [piece, pltpu.roll(piece, 96, 1)]
+            sides.append(jnp.concatenate(pieces, axis=0))
+        before, after = sides
         wide_rows = jnp.concatenate(
             [jnp.where(lane < HALF, before, middle), jnp.where(lane < HALF, middle, after)],
             axis=1,
@@ -554,7 +574,9 @@
         + [
             pltpu.VMEM((32, COLS), F32),
             pltpu.VMEM((32, COLS), BF16),
-            pltpu.VMEM((3, 160, COLS), BF16),
+            pltpu.VMEM((16, COLS), BF16),
+            pltpu.VMEM((160, COLS), BF16),
+            pltpu.VMEM((2, 80, COLS), BF16),
             pltpu.VMEM((5, 2, 256, 256), BF16),
             pltpu.VMEM((9, 256, 256), BF16),
             pltpu.VMEM((9, 128, 256), BF16),

time: 20.4 us -> 20.5 us (level)
  no operation moved by 1% of the time
where the time goes in v5:
time: 20.5 us; the launch traced here: 20.4 us
  Pallas kernels  19.7 us (96%)
  local copies, waits for them, and re-layouts  0.62 us (3%)
    pallas_call x1, Pallas kernels, per_device(): pl.pallas_call(functools.partial(kernel, n_wide, n_narrow), out_shape=jax...  19.7 us
    unnamed x1, local copies, waits for them, and re-layouts  0.62 us

profile of v5, /device:TPU:71, one launch (start us, length us, event | category | flops | bytes accessed | tf_op | source)
XLA Modules:
  0.0 20.4 jit_solution(9873920986175474752)
XLA Ops:
  0.0 19.7 %unet.1 = f32[64,128]{1,0:T(8,128)S(1)} custom-call(bf16[8,4,128]{2,1,0:T(4,128)(2,1)} %bitcast.6, bf16[27,32]{1,0:T(8,128)(2,1)} %bitcast.7, bf16[27,32,32]{2,1,0:T(8,128)(2,1)} %w_encode.1, bf16[27,32,64]{2,1,0:T(8,128)(2,1)} %bitcast.5, bf16[27,64,64]{2,1,0:T(8,128)(2,1)} %w_deep.1, bf16[8,32,64]{2,1,0:T(8,128)(2,1)} %w_upward.1, ...), custom_call_target="tpu_custom_call" | custom-call | tf_op jit(solution)/shard_map/unet/pallas_call | solution.py:568
  19.7 0.6 %copy.21 = f32[2,8,4,128]{3,2,1,0:T(4,128)} copy(f32[2,8,4,128]{3,2,1,0:T(4,128)S(1)} %bitcast.4) | data formatting | bytes 65536
